TPU v7x, 32 devices: a whole 2x2x4 slice. The times are simulated.
32 devices in a mesh: expert: 16 (over z, y, core), shard: 2 (over x).
Axes of the slice: x: 2, y: 2, z: 4, core: 2. Of those that a mesh axis runs over, the one named last changes fastest.
Arguments:
- tokens: bfloat16 [4096, 2048], P(('expert', 'shard')), may hold values from -6 to 6
- cotangent: bfloat16 [4096, 2048], P(('expert', 'shard')), may hold values from -6 to 6
- routes: int32 [4096, 6], P(('expert', 'shard')), may hold values from 0 to 15, all different within a row; in each aligned block of 128 rows (0 to 127, 128 to 255, ...) at most 64 rows name the same one
- lengths: int32 [16, 3], P('expert'), may hold values from 1 to 128, 256 in all within a row
- doc_order: int32 [16, 3], P('expert'), may hold values from 0 to 2, each once within a row
- attn_gain: float32 [2048], P('shard'), may hold values from 0.25 to 1.75
- query_proj: float32 [2048, 3072], P('shard'), may hold values from -0.125 to 0.125
- latent_proj: float32 [2048, 576], P('shard'), may hold values from -0.125 to 0.125
- latent_gain: float32 [512], P('shard'), may hold values from 0.25 to 1.75
- expand_proj: float32 [512, 4096], P('shard'), may hold values from -0.25 to 0.25
- output_proj: float32 [2048, 2048], P('shard'), may hold values from -0.5 to 0.5
- ffn_gain: float32 [2048], P('shard'), may hold values from 0.25 to 1.75
- router_proj: float32 [2048, 16], P('shard'), may hold values from -0.0625 to 0.0625
- shared_gate: float32 [2048, 1408], P('shard'), may hold values from -0.125 to 0.125
- shared_up: float32 [2048, 1408], P('shard'), may hold values from -0.125 to 0.125
- shared_down: float32 [1408, 2048], P('shard'), may hold values from -0.3125 to 0.3125
- expert_gate: float32 [16, 2048, 1408], P('expert', 'shard'), may hold values from -0.125 to 0.125
- expert_up: float32 [16, 2048, 1408], P('expert', 'shard'), may hold values from -0.125 to 0.125
- expert_down: float32 [16, 1408, 2048], P('expert', 'shard'), may hold values from -0.4375 to 0.4375
Outputs:
- layer_out: float32 [4096, 2048], P(('expert', 'shard'))
- grad_tokens: float32 [4096, 2048], P(('expert', 'shard'))
- grad_attn_gain: float32 [2048], P(('expert', 'shard'))
- grad_query_proj: float32 [2048, 3072], P(('expert', 'shard'))
- grad_latent_proj: float32 [2048, 576], P(('expert', 'shard'))
- grad_latent_gain: float32 [512], P(('expert', 'shard'))
- grad_expand_proj: float32 [512, 4096], P(('expert', 'shard'))
- grad_output_proj: float32 [2048, 2048], P(('expert', 'shard'))
- grad_ffn_gain: float32 [2048], P(('expert', 'shard'))
- grad_router_proj: float32 [2048, 16], P(('expert', 'shard'))
- grad_shared_gate: float32 [2048, 1408], P(('expert', 'shard'))
- grad_shared_up: float32 [2048, 1408], P(('expert', 'shard'))
- grad_shared_down: float32 [1408, 2048], P(('expert', 'shard'))
- grad_expert_gate: float32 [16, 2048, 1408], P('expert', 'shard')
- grad_expert_up: float32 [16, 2048, 1408], P('expert', 'shard')
- grad_expert_down: float32 [16, 1408, 2048], P('expert', 'shard')
Inputs may be any that keep to these rules, and one draw needn't show every extreme that they name: `routes`: each row names 6 different experts; among the 128 rows of one device no expert is named more than 64 times, and on some device one expert is named exactly 64 times. `lengths`: each row sums to 256, and its largest entry is exactly 128. `doc_order`: each row is a permutation of 0 to 2.
All inputs are finite; a program needn't handle non-finite values.
Results may differ from a plain program's by a relative error of at most 0.018.
The roundings to bfloat16 on the way count: a program that leaves them out, or rounds other values in their place, can miss the bound.
Values may be sent and summed in bfloat16 or wider, within the bound.
A program may use at most 448 MiB of HBM per device.

v0:
```python
import math

import jax
import jax.numpy as jnp
from jax import lax
from jax.sharding import PartitionSpec as P

D = 2048
HEADS = 16
NOPE_DIM = 128
ROPE_DIM = 64
LATENT = 512
V_DIM = 128


norm_eps = 1e-06
masked_score = -1e30


def rms_scale(values, gain_vec):
    return (
        values * lax.rsqrt(jnp.mean(values * values, axis=-1, keepdims=True) + norm_eps) * gain_vec
    )


def rotate(values, cosine, sine_vals):
    half_width = values.shape[-1] // 2
    front_part = values[..., :half_width]
    back_part = values[..., half_width:]
    return jnp.concatenate(
        [front_part * cosine - back_part * sine_vals, back_part * cosine + front_part * sine_vals],
        axis=-1,
    )


def swish_act(values):
    return values / (1.0 + jnp.exp(-values))


def swish_slope(values):
    sigmoid_vals = 1.0 / (1.0 + jnp.exp(-values))
    return sigmoid_vals * (1.0 + values * (1.0 - sigmoid_vals))


def doc_layout(lengths_row, order_row, count):
    seq_slots = jnp.arange(lengths_row.shape[0], dtype=jnp.int32)
    picked = jnp.sum(
        jnp.where(order_row[:, None] == seq_slots[None, :], lengths_row[None, :], 0), axis=1
    )
    seq_ends = jnp.cumsum(picked)
    seq_starts = seq_ends - picked
    places = jnp.arange(count, dtype=jnp.int32)
    segment = jnp.sum((places[:, None] >= seq_ends[None, :]).astype(jnp.int32), axis=1)
    seq_begin = jnp.sum(
        jnp.where(segment[:, None] == seq_slots[None, :], seq_starts[None, :], 0), axis=1
    )
    return (places - seq_begin, segment)


def rope_tables(position, width):
    half_width = width // 2
    frequency = jnp.exp(
        -(2.0 * jnp.arange(half_width, dtype=jnp.float32) / width) * math.log(10000.0)
    )
    angles = position.astype(jnp.float32)[:, None] * frequency[None, :]
    return (jnp.cos(angles), jnp.sin(angles))


def body(
    tokens,
    cotangent,
    routes,
    lengths,
    doc_order,
    attn_gain,
    query_proj,
    latent_proj,
    latent_gain,
    expand_proj,
    output_proj,
    ffn_gain,
    router_proj,
    shared_gate,
    shared_up,
    shared_down,
    expert_gate,
    expert_up,
    expert_down,
):
    half_type = jnp.bfloat16
    full_type = jnp.float32
    tok_rows = tokens.shape[0]
    group_rows = tok_rows * lax.axis_size("shard")
    experts_all = router_proj.shape[1]
    top_count = routes.shape[1]
    capacity = min(tok_rows, 4 * tok_rows * top_count // (3 * experts_all))
    local_experts = expert_gate.shape[0]
    score_scale = 1.0 / math.sqrt(NOPE_DIM + ROPE_DIM)
    (
        attn_gain_w,
        query_w,
        latent_w,
        latent_gain_w,
        expand_w,
        output_w,
        ffn_gain_w,
        router_w,
        shared_gate_w,
        shared_up_w,
        shared_down_w,
    ) = (
        lax.all_gather(attn_gain.astype(half_type), "shard", axis=0, tiled=True),
        lax.all_gather(query_proj.astype(half_type), "shard", axis=0, tiled=True),
        lax.all_gather(latent_proj.astype(half_type), "shard", axis=0, tiled=True),
        lax.all_gather(latent_gain.astype(half_type), "shard", axis=0, tiled=True),
        lax.all_gather(expand_proj.astype(half_type), "shard", axis=0, tiled=True),
        lax.all_gather(output_proj.astype(half_type), "shard", axis=0, tiled=True),
        lax.all_gather(ffn_gain.astype(half_type), "shard", axis=0, tiled=True),
        lax.all_gather(router_proj.astype(half_type), "shard", axis=0, tiled=True),
        lax.all_gather(shared_gate.astype(half_type), "shard", axis=0, tiled=True),
        lax.all_gather(shared_up.astype(half_type), "shard", axis=0, tiled=True),
        lax.all_gather(shared_down.astype(half_type), "shard", axis=0, tiled=True),
    )
    gate_full, up_full, down_full = (
        lax.all_gather(expert_gate.astype(half_type), "shard", axis=1, tiled=True),
        lax.all_gather(expert_up.astype(half_type), "shard", axis=1, tiled=True),
        lax.all_gather(expert_down.astype(half_type), "shard", axis=1, tiled=True),
    )
    row_start = lax.axis_index("shard") * tok_rows
    position, segment = doc_layout(lengths[0], doc_order[0], group_rows)
    cosine_all, sine_all = rope_tables(position, ROPE_DIM)
    cosine_own = lax.dynamic_slice_in_dim(cosine_all, row_start, tok_rows, 0)
    sine_own = lax.dynamic_slice_in_dim(sine_all, row_start, tok_rows, 0)
    segment_own = lax.dynamic_slice_in_dim(segment, row_start, tok_rows, 0)
    query_place = row_start + jnp.arange(tok_rows, dtype=jnp.int32)
    key_place = jnp.arange(group_rows, dtype=jnp.int32)
    visible = (segment_own[:, None] == segment[None, :]) & (
        key_place[None, :] <= query_place[:, None]
    )
    input_rows = tokens.astype(full_type)
    attn_gain_f = attn_gain_w.astype(full_type)
    latent_gain_f = latent_gain_w.astype(full_type)
    ffn_gain_f = ffn_gain_w.astype(full_type)
    normed_one = rms_scale(input_rows, attn_gain_f).astype(half_type)
    query_raw = jnp.dot(normed_one, query_w, preferred_element_type=full_type)
    latent_raw = jnp.dot(normed_one, latent_w, preferred_element_type=full_type)
    latent_vals = rms_scale(latent_raw[:, :LATENT], latent_gain_f).astype(half_type)
    key_rope = rotate(latent_raw[:, LATENT:], cosine_own, sine_own).astype(half_type)
    latent_all, key_rope_all = (
        lax.all_gather(latent_vals, "shard", axis=0, tiled=True),
        lax.all_gather(key_rope, "shard", axis=0, tiled=True),
    )
    expanded = (
        jnp.dot(latent_all, expand_w, preferred_element_type=full_type)
        .astype(half_type)
        .reshape(group_rows, HEADS, NOPE_DIM + V_DIM)
    )
    keys_all = jnp.concatenate(
        [
            expanded[:, :, :NOPE_DIM],
            jnp.broadcast_to(key_rope_all[:, None, :], (group_rows, HEADS, ROPE_DIM)),
        ],
        axis=-1,
    )
    values_all = expanded[:, :, NOPE_DIM:]
    query_heads = query_raw.reshape(tok_rows, HEADS, NOPE_DIM + ROPE_DIM)
    queries = jnp.concatenate(
        [
            query_heads[:, :, :NOPE_DIM],
            rotate(query_heads[:, :, NOPE_DIM:], cosine_own[:, None, :], sine_own[:, None, :]),
        ],
        axis=-1,
    ).astype(half_type)
    scores = (
        jnp.einsum("qhd,khd->hqk", queries, keys_all, preferred_element_type=full_type)
        * score_scale
    )
    scores = jnp.where(visible[None], scores, masked_score)
    top_score = jnp.max(scores, axis=-1, keepdims=True)
    log_total = top_score + jnp.log(jnp.sum(jnp.exp(scores - top_score), axis=-1, keepdims=True))
    attn_probs = jnp.exp(scores - log_total)
    attended = (
        jnp.einsum(
            "hqk,khd->qhd",
            attn_probs.astype(half_type),
            values_all,
            preferred_element_type=full_type,
        )
        .astype(half_type)
        .reshape(tok_rows, HEADS * V_DIM)
    )
    resid = input_rows + jnp.dot(attended, output_w, preferred_element_type=full_type)
    normed_two = rms_scale(resid, ffn_gain_f).astype(half_type)
    logits = jnp.dot(normed_two, router_w, preferred_element_type=full_type)
    expert_ids = jnp.arange(experts_all, dtype=jnp.int32)
    chosen_mask = routes[:, :, None] == expert_ids[None, None, :]
    chosen = jnp.sum(jnp.where(chosen_mask, logits[:, None, :], 0.0), axis=-1)
    gate_top = jnp.max(chosen, axis=-1, keepdims=True)
    gate_exp = jnp.exp(chosen - gate_top)
    gates = gate_exp / jnp.sum(gate_exp, axis=-1, keepdims=True)
    shared_pre = jnp.dot(normed_two, shared_gate_w, preferred_element_type=full_type)
    shared_lin = jnp.dot(normed_two, shared_up_w, preferred_element_type=full_type)
    shared_act = (swish_act(shared_pre) * shared_lin).astype(half_type)
    shared_out = jnp.dot(shared_act, shared_down_w, preferred_element_type=full_type)
    flat_ids = routes.reshape(-1)
    onehot = (flat_ids[:, None] == expert_ids[None, :]).astype(jnp.int32)
    running = jnp.cumsum(onehot, axis=0)
    slot_index = jnp.sum(onehot * running, axis=1) - 1
    target = flat_ids * capacity + slot_index
    token_copies = jnp.repeat(normed_two, top_count, axis=0)
    outbound = (
        jnp.zeros((experts_all * capacity, D), half_type)
        .at[target]
        .set(token_copies)
        .reshape(experts_all, capacity, D)
    )
    arrived = lax.all_to_all(outbound, "expert", split_axis=0, concat_axis=0, tiled=True)
    grouped = arrived.reshape(-1, local_experts, arrived.shape[1], D)
    pre_gate = jnp.einsum("nekd,edf->nekf", grouped, gate_full, preferred_element_type=full_type)
    lin_part = jnp.einsum("nekd,edf->nekf", grouped, up_full, preferred_element_type=full_type)
    act_vals = (swish_act(pre_gate) * lin_part).astype(half_type)
    expert_built = jnp.einsum(
        "nekf,efd->nekd", act_vals, down_full, preferred_element_type=full_type
    ).astype(half_type)
    produced = expert_built.reshape(arrived.shape)
    returned = lax.all_to_all(produced, "expert", split_axis=0, concat_axis=0, tiled=True)
    returned_rows = (
        returned.reshape(experts_all * capacity, D)[target]
        .astype(full_type)
        .reshape(tok_rows, top_count, D)
    )
    mixture = jnp.sum(gates[:, :, None] * returned_rows, axis=1)
    layer_out = resid + mixture + shared_out
    query_b, latent_b, expand_b, output_b, router_b, shared_gate_b, shared_up_b, shared_down_b = (
        lax.all_gather(query_proj.astype(half_type), "shard", axis=0, tiled=True),
        lax.all_gather(latent_proj.astype(half_type), "shard", axis=0, tiled=True),
        lax.all_gather(expand_proj.astype(half_type), "shard", axis=0, tiled=True),
        lax.all_gather(output_proj.astype(half_type), "shard", axis=0, tiled=True),
        lax.all_gather(router_proj.astype(half_type), "shard", axis=0, tiled=True),
        lax.all_gather(shared_gate.astype(half_type), "shard", axis=0, tiled=True),
        lax.all_gather(shared_up.astype(half_type), "shard", axis=0, tiled=True),
        lax.all_gather(shared_down.astype(half_type), "shard", axis=0, tiled=True),
    )
    gate_back, up_back, down_back = (
        lax.all_gather(expert_gate.astype(half_type), "shard", axis=1, tiled=True),
        lax.all_gather(expert_up.astype(half_type), "shard", axis=1, tiled=True),
        lax.all_gather(expert_down.astype(half_type), "shard", axis=1, tiled=True),
    )
    upstream = cotangent.astype(full_type)
    gate_grad = jnp.sum(upstream[:, None, :] * returned_rows, axis=-1)
    mix_grad = (gates[:, :, None] * upstream[:, None, :]).astype(half_type).reshape(-1, D)
    outbound_grad = (
        jnp.zeros((experts_all * capacity, D), half_type)
        .at[target]
        .set(mix_grad)
        .reshape(experts_all, capacity, D)
    )
    arrived_grad = lax.all_to_all(outbound_grad, "expert", split_axis=0, concat_axis=0, tiled=True)
    grouped = arrived.reshape(-1, local_experts, capacity, D)
    grouped_grad = arrived_grad.reshape(-1, local_experts, capacity, D)
    pre_gate = jnp.einsum("nekd,edf->nekf", grouped, gate_back, preferred_element_type=full_type)
    lin_part = jnp.einsum("nekd,edf->nekf", grouped, up_back, preferred_element_type=full_type)
    act_vals = (swish_act(pre_gate) * lin_part).astype(half_type)
    grad_down_e = jnp.einsum(
        "nekf,nekd->efd", act_vals, grouped_grad, preferred_element_type=full_type
    )
    act_grad = jnp.einsum(
        "nekd,efd->nekf", grouped_grad, down_back, preferred_element_type=full_type
    )
    pre_grad = (act_grad * lin_part * swish_slope(pre_gate)).astype(half_type)
    lin_grad = (act_grad * swish_act(pre_gate)).astype(half_type)
    grad_gate_e = jnp.einsum("nekd,nekf->edf", grouped, pre_grad, preferred_element_type=full_type)
    grad_up_e = jnp.einsum("nekd,nekf->edf", grouped, lin_grad, preferred_element_type=full_type)
    rows_grad = jnp.einsum(
        "nekf,edf->nekd", pre_grad, gate_back, preferred_element_type=full_type
    ) + jnp.einsum("nekf,edf->nekd", lin_grad, up_back, preferred_element_type=full_type)
    rows_grad = rows_grad.astype(half_type).reshape(arrived_grad.shape)
    sent_back = lax.all_to_all(rows_grad, "expert", split_axis=0, concat_axis=0, tiled=True)
    expert_grads = (
        lax.psum_scatter(
            grad_gate_e.astype(jnp.bfloat16), "shard", scatter_dimension=1, tiled=True
        ).astype(jnp.float32),
        lax.psum_scatter(
            grad_up_e.astype(jnp.bfloat16), "shard", scatter_dimension=1, tiled=True
        ).astype(jnp.float32),
        lax.psum_scatter(
            grad_down_e.astype(jnp.bfloat16), "shard", scatter_dimension=1, tiled=True
        ).astype(jnp.float32),
    )
    normed_grad = jnp.sum(
        sent_back.reshape(experts_all * capacity, D)[target]
        .astype(full_type)
        .reshape(tok_rows, top_count, D),
        axis=1,
    )
    mean_term = jnp.sum(gates * gate_grad, axis=-1, keepdims=True)
    logit_part = gates * (gate_grad - mean_term)
    logits_grad = jnp.sum(jnp.where(chosen_mask, logit_part[:, :, None], 0.0), axis=1).astype(
        half_type
    )
    grad_router = jnp.einsum("td,te->de", normed_two, logits_grad, preferred_element_type=full_type)
    normed_grad = normed_grad + jnp.einsum(
        "te,de->td", logits_grad, router_b, preferred_element_type=full_type
    )
    shared_grad = upstream.astype(half_type)
    grad_shared_down = jnp.einsum(
        "tf,td->fd", shared_act, shared_grad, preferred_element_type=full_type
    )
    shared_act_grad = jnp.einsum(
        "td,fd->tf", shared_grad, shared_down_b, preferred_element_type=full_type
    )
    shared_pre_grad = (shared_act_grad * shared_lin * swish_slope(shared_pre)).astype(half_type)
    shared_lin_grad = (shared_act_grad * swish_act(shared_pre)).astype(half_type)
    grad_shared_gate = jnp.einsum(
        "td,tf->df", normed_two, shared_pre_grad, preferred_element_type=full_type
    )
    grad_shared_up = jnp.einsum(
        "td,tf->df", normed_two, shared_lin_grad, preferred_element_type=full_type
    )
    normed_grad = normed_grad + jnp.einsum(
        "tf,df->td", shared_pre_grad, shared_gate_b, preferred_element_type=full_type
    )
    normed_grad = normed_grad + jnp.einsum(
        "tf,df->td", shared_lin_grad, shared_up_b, preferred_element_type=full_type
    )
    _, second_pull = jax.vjp(rms_scale, resid, ffn_gain_f)
    resid_part, gain_ffn_grad = second_pull(normed_grad)
    resid_grad = upstream + resid_part
    out_grad = resid_grad.astype(half_type)
    grad_output = jnp.einsum("tv,td->vd", attended, out_grad, preferred_element_type=full_type)
    attended_grad = (
        jnp.einsum("td,vd->tv", out_grad, output_b, preferred_element_type=full_type)
        .astype(half_type)
        .reshape(tok_rows, HEADS, V_DIM)
    )
    scores_again = (
        jnp.einsum("qhd,khd->hqk", queries, keys_all, preferred_element_type=full_type)
        * score_scale
    )
    scores_again = jnp.where(visible[None], scores_again, masked_score)
    probs_again = jnp.exp(scores_again - log_total)
    prob_grad = jnp.einsum(
        "qhd,khd->hqk", attended_grad, values_all, preferred_element_type=full_type
    )
    row_term = jnp.sum(probs_again * prob_grad, axis=-1, keepdims=True)
    score_grad = (probs_again * (prob_grad - row_term) * score_scale).astype(half_type)
    query_grad = jnp.einsum("hqk,khd->qhd", score_grad, keys_all, preferred_element_type=full_type)
    key_grad = jnp.einsum("hqk,qhd->khd", score_grad, queries, preferred_element_type=full_type)
    value_grad = jnp.einsum(
        "hqk,qhd->khd",
        probs_again.astype(half_type),
        attended_grad,
        preferred_element_type=full_type,
    )
    expanded_grad = jnp.concatenate([key_grad[:, :, :NOPE_DIM], value_grad], axis=-1).reshape(
        group_rows, HEADS * (NOPE_DIM + V_DIM)
    )
    rope_grad = jnp.sum(key_grad[:, :, NOPE_DIM:], axis=1)
    expanded_own, rope_own = (
        lax.psum_scatter(
            expanded_grad.astype(jnp.bfloat16), "shard", scatter_dimension=0, tiled=True
        ).astype(jnp.float32),
        lax.psum_scatter(
            rope_grad.astype(jnp.bfloat16), "shard", scatter_dimension=0, tiled=True
        ).astype(jnp.float32),
    )
    expanded_low = expanded_own.astype(half_type)
    grad_expand = jnp.einsum(
        "tc,tk->ck", latent_vals, expanded_low, preferred_element_type=full_type
    )
    latent_grad = jnp.einsum("tk,ck->tc", expanded_low, expand_b, preferred_element_type=full_type)
    _, latent_pull = jax.vjp(rms_scale, latent_raw[:, :LATENT], latent_gain_f)
    clatent_grad, gain_latent_grad = latent_pull(latent_grad)
    _, krope_pull = jax.vjp(rotate, latent_raw[:, LATENT:], cosine_own, sine_own)
    krope_grad = krope_pull(rope_own)[0]
    latent_raw_grad = jnp.concatenate([clatent_grad, krope_grad], axis=-1).astype(half_type)
    _, qrope_pull = jax.vjp(
        rotate, query_heads[:, :, NOPE_DIM:], cosine_own[:, None, :], sine_own[:, None, :]
    )
    qrope_grad = qrope_pull(query_grad[:, :, NOPE_DIM:])[0]
    query_raw_grad = (
        jnp.concatenate([query_grad[:, :, :NOPE_DIM], qrope_grad], axis=-1)
        .reshape(tok_rows, HEADS * (NOPE_DIM + ROPE_DIM))
        .astype(half_type)
    )
    grad_query = jnp.einsum(
        "td,tq->dq", normed_one, query_raw_grad, preferred_element_type=full_type
    )
    grad_latent = jnp.einsum(
        "td,tq->dq", normed_one, latent_raw_grad, preferred_element_type=full_type
    )
    first_grad = jnp.einsum(
        "tq,dq->td", query_raw_grad, query_b, preferred_element_type=full_type
    ) + jnp.einsum("tq,dq->td", latent_raw_grad, latent_b, preferred_element_type=full_type)
    _, first_pull = jax.vjp(rms_scale, input_rows, attn_gain_f)
    input_part, gain_attn_grad = first_pull(first_grad)
    tokens_grad = resid_grad + input_part
    dense_sums = (
        lax.psum_scatter(gain_attn_grad, ("expert", "shard"), scatter_dimension=0, tiled=True),
        lax.psum_scatter(grad_query, ("expert", "shard"), scatter_dimension=0, tiled=True),
        lax.psum_scatter(grad_latent, ("expert", "shard"), scatter_dimension=0, tiled=True),
        lax.psum_scatter(gain_latent_grad, ("expert", "shard"), scatter_dimension=0, tiled=True),
        lax.psum_scatter(grad_expand, ("expert", "shard"), scatter_dimension=0, tiled=True),
        lax.psum_scatter(grad_output, ("expert", "shard"), scatter_dimension=0, tiled=True),
        lax.psum_scatter(gain_ffn_grad, ("expert", "shard"), scatter_dimension=0, tiled=True),
        lax.psum_scatter(grad_router, ("expert", "shard"), scatter_dimension=0, tiled=True),
        lax.psum_scatter(grad_shared_gate, ("expert", "shard"), scatter_dimension=0, tiled=True),
        lax.psum_scatter(grad_shared_up, ("expert", "shard"), scatter_dimension=0, tiled=True),
        lax.psum_scatter(grad_shared_down, ("expert", "shard"), scatter_dimension=0, tiled=True),
    )
    return (
        layer_out,
        tokens_grad,
        dense_sums[0],
        dense_sums[1],
        dense_sums[2],
        dense_sums[3],
        dense_sums[4],
        dense_sums[5],
        dense_sums[6],
        dense_sums[7],
        dense_sums[8],
        dense_sums[9],
        dense_sums[10],
        expert_grads[0],
        expert_grads[1],
        expert_grads[2],
    )


def solution(mesh):
    return jax.shard_map(
        body,
        mesh=mesh,
        in_specs=(
            P(("expert", "shard"), None),
            P(("expert", "shard"), None),
            P(("expert", "shard"), None),
            P("expert", None),
            P("expert", None),
            P("shard"),
            P("shard", None),
            P("shard", None),
            P("shard"),
            P("shard", None),
            P("shard", None),
            P("shard"),
            P("shard", None),
            P("shard", None),
            P("shard", None),
            P("shard", None),
            P("expert", "shard", None),
            P("expert", "shard", None),
            P("expert", "shard", None),
        ),
        out_specs=(
            P(("expert", "shard"), None),
            P(("expert", "shard"), None),
            P(("expert", "shard")),
            P(("expert", "shard"), None),
            P(("expert", "shard"), None),
            P(("expert", "shard")),
            P(("expert", "shard"), None),
            P(("expert", "shard"), None),
            P(("expert", "shard")),
            P(("expert", "shard"), None),
            P(("expert", "shard"), None),
            P(("expert", "shard"), None),
            P(("expert", "shard"), None),
            P("expert", "shard", None),
            P("expert", "shard", None),
            P("expert", "shard", None),
        ),
        check_vma=False,
    )
```

profile of v0, /device:TPU:11, one launch (start us, length us, event | category | flops | bytes accessed | tf_op | source)
XLA Modules:
  0.0 2973.0 jit_solution(7648561963770156333)
XLA Ops:
  81.2 28.2 all-gather.14.cloned.1.call-done
  118.6 144.9 %all-gather.16.cloned.1.call-done = bf16[2048,3072]{1,0:T(8,128)(2,1)} async-done(((bf16[1024,3072]{1,0:T(8,128)(2,1)}), bf16[2048,3072]{1,0:T(8,128)(2,1)}) %all-gather.16.cloned.1.call-update) | async-done | bytes 12582928 | tf_op jit(solution)/shard_map/all_gather | solution.py:113
  275.6 94.0 %all-gather.18.cloned.1.call-done = bf16[2048,2048]{1,0:T(8,128)(2,1)} async-done(((bf16[1024,2048]{1,0:T(8,128)(2,1)}), bf16[2048,2048]{1,0:T(8,128)(2,1)}) %all-gather.18.cloned.1.call-update) | async-done | bytes 8388624 | tf_op jit(solution)/shard_map/all_gather | solution.py:117
  376.3 15.4 scatter_custom_fusion.1
  422.5 66.1 %all-to-all-done.2 = bf16[16,64,2048]{2,1,0:T(8,128)(2,1)} async-done(((bf16[16,64,2048]{2,1,0:T(8,128)(2,1)}), bf16[16,64,2048]{2,1,0:T(8,128)(2,1)}, u32[]{:S(2)}, u32[]{:S(2)}) %all-to-all-start.2) | async-done | bytes 4194336 | tf_op jit(solution)/shard_map/all_to_all | solution.py:258
  504.8 11.8 fusion.9
  521.3 64.6 %all-to-all-done = bf16[16,64,2048]{2,1,0:T(8,128)(2,1)} async-done(((bf16[16,64,2048]{2,1,0:T(8,128)(2,1)}), bf16[16,64,2048]{2,1,0:T(8,128)(2,1)}, u32[]{:S(2)}, u32[]{:S(2)}) %all-to-all-start) | async-done | bytes 4194336 | tf_op jit(solution)/shard_map/all_to_all | solution.py:217
  585.9 11.7 fusion.15
  597.6 15.6 fusion.6
  614.9 11.2 fusion.26
  658.7 64.6 %all-to-all-done.1 = bf16[16,64,2048]{2,1,0:T(8,128)(2,1)} async-done(((bf16[16,64,2048]{2,1,0:T(8,128)(2,1)}), bf16[16,64,2048]{2,1,0:T(8,128)(2,1)}, u32[]{:S(2)}, u32[]{:S(2)}) %all-to-all-start.1) | async-done | bytes 4194336 | tf_op jit(solution)/shard_map/all_to_all | solution.py:226
  738.9 11.2 all-gather.28.cloned.1.call-done
  754.6 72.0 %all-gather.30.cloned.1.call-done = bf16[1408,2048]{1,0:T(8,128)(2,1)} async-done(((bf16[704,2048]{1,0:T(8,128)(2,1)}), bf16[1408,2048]{1,0:T(8,128)(2,1)}) %all-gather.30.cloned.1.call-update) | async-done | bytes 5767184 | tf_op jit(solution)/shard_map/all_gather | solution.py:122
  901.4 16.8 convolution_bitcast_fusion
  994.0 16.5 fusion.48
  1040.5 457.2 %fusion = f32[48,2048]{1,0:T(8,128)S(1)} fusion(f32[1408,2048]{1,0:T(8,128)} %fusion.117), kind=kCustom, calls=%all-reduce-scatter | all-reduce-scatter fusion | flops 3145729 | bytes 11927552
  1507.9 11.2 collective-permute-done.2
  1562.4 54.0 %all-reduce.9 = (f32[2048]{0:T(1024)S(1)}, f32[512]{0:T(512)S(1)}, f32[2048]{0:T(1024)S(1)}) all-reduce(f32[2048]{0:T(1024)S(1)} %get-tuple-element.20, f32[512]{0:T(512)S(1)} %get-tuple-element.22, f32[2048]{0:T(1024)S(1)} %copy-done.40), channel_id=4, replica_groups=mesh['expert'=16,'shard'=2] {'expert','shard'}, use_global_device_ids=true, to_apply=%region_30.31.clone | all-reduce | flops 4608 | bytes 36864
  1620.7 141.3 %reduce-scatter.29.cloned.1.call-done = f32[64,1408]{1,0:T(8,128)} async-done(((f32[2048,1408]{1,0:T(8,128)}), f32[64,1408]{1,0:T(8,128)}) %reduce-scatter.29.cloned.1.call-update) | async-done | bytes 360464 | tf_op jit(solution)/shard_map/reduce_scatter | solution.py:407
  1762.0 256.8 %reduce-scatter.31.cloned.1.call-done = f32[64,1408]{1,0:T(8,128)} async-done(((f32[2048,1408]{1,0:T(8,128)}), f32[64,1408]{1,0:T(8,128)}) %reduce-scatter.31.cloned.1.call-update) | async-done | bytes 360464 | tf_op jit(solution)/shard_map/reduce_scatter | solution.py:408
  2018.8 130.0 %reduce-scatter.23.cloned.1.call-done = f32[64,576]{1,0:T(8,128)} async-done(((f32[2048,576]{1,0:T(8,128)}), f32[64,576]{1,0:T(8,128)}) %reduce-scatter.23.cloned.1.call-update) | async-done | bytes 147472 | tf_op jit(solution)/shard_map/reduce_scatter | solution.py:401
  2148.8 202.4 %reduce-scatter.25.cloned.1.call-done = f32[16,4096]{1,0:T(8,128)} async-done(((f32[512,4096]{1,0:T(8,128)}), f32[16,4096]{1,0:T(8,128)}) %reduce-scatter.25.cloned.1.call-update) | async-done | bytes 262160 | tf_op jit(solution)/shard_map/reduce_scatter | solution.py:403
  2351.2 252.4 %reduce-scatter.21.cloned.1.call-done = f32[64,3072]{1,0:T(8,128)} async-done(((f32[2048,3072]{1,0:T(8,128)}), f32[64,3072]{1,0:T(8,128)}) %reduce-scatter.21.cloned.1.call-update) | async-done | bytes 786448 | tf_op jit(solution)/shard_map/reduce_scatter | solution.py:400
  2603.6 362.5 %reduce-scatter.27.cloned.1.call-done = f32[64,2048]{1,0:T(8,128)} async-done(((f32[2048,2048]{1,0:T(8,128)}), f32[64,2048]{1,0:T(8,128)}) %reduce-scatter.27.cloned.1.call-update) | async-done | bytes 524304 | tf_op jit(solution)/shard_map/reduce_scatter | solution.py:404
  (351 shorter events, 445.2 us)
Async XLA Ops:
  10.1 99.3 %all-gather.14.cloned.1.call-start = ((), (), s32[]{:S(2)}) async-start(), calls=%async_computation.17 | async-start | bytes 6291456 | tf_op jit(solution)/shard_map/all_gather | solution.py:116
  14.0 249.6 %all-gather.16.cloned.1.call-start = ((), (), s32[]{:S(2)}) async-start(), calls=%async_computation.18 | async-start | bytes 18874368 | tf_op jit(solution)/shard_map/all_gather | solution.py:113
  22.5 347.1 %all-gather.18.cloned.1.call-start = ((), (), s32[]{:S(2)}) async-start(), calls=%async_computation.19 | async-start | bytes 12582912 | tf_op jit(solution)/shard_map/all_gather | solution.py:117
  28.7 476.1 %all-gather.24.cloned.1.call-start = ((), (), s32[]{:S(2)}) async-start(), calls=%async_computation.22 | async-start | bytes 8650752 | tf_op jit(solution)/shard_map/all_gather | solution.py:127
  391.7 96.8 %all-to-all-start.2 = ((bf16[16,64,2048]{2,1,0:T(8,128)(2,1)}), bf16[16,64,2048]{2,1,0:T(8,128)(2,1)}, u32[]{:S(2)}, u32[]{:S(2)}) async-start(bf16[16,64,2048]{2,1,0:T(8,128)(2,1)} %bitcast.203), calls=%async_computation.2 | async-start | bytes 8388608 | tf_op jit(solution)/shard_map/all_to_all | solution.py:258
  398.2 123.1 %all-gather.22.cloned.1.call-start = ((), (), s32[]{:S(2)}) async-start(), calls=%async_computation.21 | async-start | bytes 8650752 | tf_op jit(solution)/shard_map/all_gather | solution.py:126
  488.5 97.4 %all-to-all-start = ((bf16[16,64,2048]{2,1,0:T(8,128)(2,1)}), bf16[16,64,2048]{2,1,0:T(8,128)(2,1)}, u32[]{:S(2)}, u32[]{:S(2)}) async-start(bf16[16,64,2048]{2,1,0:T(8,128)(2,1)} %bitcast.202), calls=%async_computation | async-start | bytes 8388608 | tf_op jit(solution)/shard_map/all_to_all | solution.py:217
  495.6 102.0 %all-gather.20.cloned.1.call-start = ((), (), s32[]{:S(2)}) async-start(), calls=%async_computation.20 | async-start | bytes 8650752 | tf_op jit(solution)/shard_map/all_gather | solution.py:125
  500.2 235.0 %all-gather.26.cloned.1.call-start = ((), (), s32[]{:S(2)}) async-start(), calls=%async_computation.23 | async-start | bytes 8650752 | tf_op jit(solution)/shard_map/all_gather | solution.py:120
  626.1 97.1 %all-to-all-start.1 = ((bf16[16,64,2048]{2,1,0:T(8,128)(2,1)}), bf16[16,64,2048]{2,1,0:T(8,128)(2,1)}, u32[]{:S(2)}, u32[]{:S(2)}) async-start(bf16[16,64,2048]{2,1,0:T(8,128)(2,1)} %fusion.26), calls=%async_computation.1 | async-start | bytes 8388608 | tf_op jit(solution)/shard_map/all_to_all | solution.py:226
  632.9 117.1 %all-gather.28.cloned.1.call-start = ((), (), s32[]{:S(2)}) async-start(), calls=%async_computation.24 | async-start | bytes 8650752 | tf_op jit(solution)/shard_map/all_gather | solution.py:121
  723.3 125.3 %all-to-all-start.3 = ((bf16[16,64,2048]{2,1,0:T(8,128)(2,1)}), bf16[16,64,2048]{2,1,0:T(8,128)(2,1)}, u32[]{:S(2)}, u32[]{:S(2)}) async-start(bf16[16,64,2048]{2,1,0:T(8,128)(2,1)} %add_convert_fusion), calls=%async_computation.3 | async-start | bytes 8388608 | tf_op jit(solution)/shard_map/all_to_all | solution.py:278
  730.3 96.2 %all-gather.30.cloned.1.call-start = ((), (), s32[]{:S(2)}) async-start(), calls=%async_computation.25 | async-start | bytes 8650752 | tf_op jit(solution)/shard_map/all_gather | solution.py:122
  735.1 243.2 %reduce-scatter.41.cloned.1.call-start = ((), (), s32[]{:S(2)}) async-start(), calls=%async_computation.36 | async-start | bytes 98304
  930.4 614.0 %reduce-scatter.43.cloned.1.call-start = ((), (), s32[]{:S(2)}) async-start(), calls=%async_computation.37 | async-start | bytes 1081344
  931.9 614.0 %reduce-scatter.33.cloned.1.call-start = ((), (), s32[]{:S(2)}) async-start(), calls=%async_computation.32 | async-start | bytes 8650752 | tf_op jit(solution)/shard_map/reduce_scatter | solution.py:280
  942.9 607.7 %reduce-scatter.35.cloned.1.call-start = ((), (), s32[]{:S(2)}) async-start(), calls=%async_computation.33 | async-start | bytes 8650752 | tf_op jit(solution)/shard_map/reduce_scatter | solution.py:283
  954.1 601.3 %reduce-scatter.37.cloned.1.call-start = ((), (), s32[]{:S(2)}) async-start(), calls=%async_computation.34 | async-start | bytes 8650752 | tf_op jit(solution)/shard_map/reduce_scatter | solution.py:286
  964.7 797.2 %reduce-scatter.29.cloned.1.call-start = ((), (), s32[]{:S(2)}) async-start(), calls=%async_computation.30 | async-start | bytes 11894784 | tf_op jit(solution)/shard_map/reduce_scatter | solution.py:407
  971.7 1047.1 %reduce-scatter.31.cloned.1.call-start = ((), (), s32[]{:S(2)}) async-start(), calls=%async_computation.31 | async-start | bytes 11894784 | tf_op jit(solution)/shard_map/reduce_scatter | solution.py:408
  978.2 1170.6 %reduce-scatter.23.cloned.1.call-start = ((), (), s32[]{:S(2)}) async-start(), calls=%async_computation.27 | async-start | bytes 5406720 | tf_op jit(solution)/shard_map/reduce_scatter | solution.py:401
  988.0 1363.2 %reduce-scatter.25.cloned.1.call-start = ((), (), s32[]{:S(2)}) async-start(), calls=%async_computation.28 | async-start | bytes 8650752 | tf_op jit(solution)/shard_map/reduce_scatter | solution.py:403
  993.9 1609.6 %reduce-scatter.21.cloned.1.call-start = ((), (), s32[]{:S(2)}) async-start(), calls=%async_computation.26 | async-start | bytes 25952256 | tf_op jit(solution)/shard_map/reduce_scatter | solution.py:400
  1024.3 1941.7 %reduce-scatter.27.cloned.1.call-start = ((), (), s32[]{:S(2)}) async-start(), calls=%async_computation.29 | async-start | bytes 17301504 | tf_op jit(solution)/shard_map/reduce_scatter | solution.py:404
  (72 other events, 2409.6 us)
Sparse Core Ops, SparseCore 0:
  10.2 36.3 all-gather.11
  48.8 60.6 all-gather.13
  111.0 152.5 all-gather.15
  265.5 104.0 all-gather.17
  370.9 74.5 all-gather.23
  446.9 74.4 all-gather.21
  522.9 74.4 all-gather.19
  599.5 74.4 all-gather.25
  675.6 74.4 all-gather.27
  752.0 74.4 all-gather.29
  923.1 9.3 reduce-scatter.40
  934.6 32.2 reduce-scatter.38
  969.3 124.8 reduce-scatter.42
  1096.9 144.9 reduce-scatter.32
  1244.7 134.7 reduce-scatter.34
  1381.7 120.8 reduce-scatter.36
  1505.4 256.4 reduce-scatter.28
  1764.8 253.8 reduce-scatter.30
  2021.7 127.0 reduce-scatter.22
  2151.6 199.4 reduce-scatter.24
  2359.3 244.1 reduce-scatter.20
  2606.4 359.5 reduce-scatter.26
where the time goes:
time: 2980 us; the launch traced here: 2970 us
  waiting for transfers between devices  1910 us (64%)
  blocking collectives  538 us (18%)
  matrix products  262 us (9%)
  other arithmetic  106 us (4%)
  local copies, waits for them, and re-layouts  105 us (4%)
  starting transfers between devices  39 us (1%)
    unnamed x2, blocking collectives  511 us
    reduce_scatter x1, waiting for transfers between devices, body(): lax.psum_scatter(grad_output, ('expert', 'shard'), scatter_dimension=0, t...  362 us
    reduce_scatter x1, waiting for transfers between devices, body(): lax.psum_scatter(grad_shared_up, ('expert', 'shard'), scatter_dimension=0...  257 us
    reduce_scatter x1, waiting for transfers between devices, body(): lax.psum_scatter(grad_query, ('expert', 'shard'), scatter_dimension=0, ti...  252 us
    reduce_scatter x1, waiting for transfers between devices, body(): lax.psum_scatter(grad_expand, ('expert', 'shard'), scatter_dimension=0, t...  202 us
    all_gather x1, waiting for transfers between devices, body(): lax.all_gather(query_proj.astype(half_type), 'shard', axis=0, tiled=True)  145 us
    reduce_scatter x1, waiting for transfers between devices, body(): lax.psum_scatter(grad_shared_gate, ('expert', 'shard'), scatter_dimension...  141 us
    reduce_scatter x1, waiting for transfers between devices, body(): lax.psum_scatter(grad_latent, ('expert', 'shard'), scatter_dimension=0, t...  130 us
  transfers between devices with their start and end apart: 29, of which 16 were waited for; matrix products, arithmetic and copies ran while one was open for 28% of the time, Pallas kernels for 0%

commit v1 on v0

v1 whole, which is shorter than its diff:
```python
import math

import jax
import jax.numpy as jnp
from jax import lax
from jax.sharding import PartitionSpec as P

HEADS = 16
NOPE_DIM = 128
ROPE_DIM = 64
LATENT = 512
V_DIM = 128
NORM_EPS = 1e-06
MASKED = -1e30
BF = jnp.bfloat16
F32 = jnp.float32
PAIR = [(0, 1), (1, 0)]


def dot(left, right, dims=((1,), (0,))):
    return lax.dot_general(left, right, (dims, ((), ())), preferred_element_type=F32)


def shard_gather(block):
    if lax.axis_size("shard") != 2:
        return lax.all_gather(block, "shard", axis=0, tiled=True)
    other = lax.ppermute(block, "shard", PAIR)
    first = lax.axis_index("shard") == 0
    return jnp.concatenate([jnp.where(first, block, other), jnp.where(first, other, block)], axis=0)


def shard_scatter(partial):
    count = lax.axis_size("shard")
    me = lax.axis_index("shard")
    rows = partial.shape[0] // count
    if count != 2:
        blocks = partial.astype(BF).reshape((count, rows) + partial.shape[1:])
        got = lax.all_to_all(blocks, "shard", split_axis=0, concat_axis=0, tiled=True)
        return jnp.sum(got.astype(F32), axis=0)
    mine = lax.dynamic_slice_in_dim(partial, me * rows, rows, 0)
    theirs = lax.dynamic_slice_in_dim(partial, (1 - me) * rows, rows, 0)
    got = lax.ppermute(theirs.astype(BF), "shard", PAIR)
    return mine.astype(F32) + got.astype(F32)


def shard_sum(partial):
    count = lax.axis_size("shard")
    if count != 2:
        return jnp.sum(lax.all_gather(partial.astype(BF), "shard").astype(F32), axis=0)
    return partial + lax.ppermute(partial.astype(BF), "shard", PAIR).astype(F32)


def shard_transpose(block):
    count = lax.axis_size("shard")
    if count != 2:
        return lax.all_to_all(block, "shard", split_axis=0, concat_axis=1, tiled=True)
    me = lax.axis_index("shard")
    rows = block.shape[0] // 2
    mine = lax.dynamic_slice_in_dim(block, me * rows, rows, 0)
    theirs = lax.dynamic_slice_in_dim(block, (1 - me) * rows, rows, 0)
    got = lax.ppermute(theirs, "shard", PAIR)
    first = me == 0
    return jnp.concatenate([jnp.where(first, mine, got), jnp.where(first, got, mine)], axis=1)


def place_halves(mine, theirs):
    me = lax.axis_index("shard")
    rows = mine.shape[0]
    full = jnp.zeros((2 * rows,) + mine.shape[1:], mine.dtype)
    full = lax.dynamic_update_slice_in_dim(full, mine, me * rows, 0)
    return lax.dynamic_update_slice_in_dim(full, theirs, (1 - me) * rows, 0)


def own_columns(weight, parts, me):
    return jnp.concatenate(
        [
            lax.dynamic_slice_in_dim(weight[i], me * width, width, 1) if width else weight[i]
            for i, width in enumerate(parts)
        ],
        axis=1,
    ).astype(BF)


def column_blocks(weights, parts):
    count = lax.axis_size("shard")
    me = lax.axis_index("shard")
    ranks = lax.axis_size("expert")
    rank = lax.axis_index("expert")
    rows = weights[0].shape[0]
    some = rows // ranks
    strip = [lax.dynamic_slice_in_dim(w, rank * some, some, 0) for w in weights]
    if count != 2:
        packed = jnp.stack([own_columns(strip, parts, s) for s in range(count)])
        crossed = lax.all_to_all(packed, "shard", split_axis=0, concat_axis=0, tiled=True)
        whole = lax.all_gather(crossed, "expert", axis=1, tiled=True)
        return whole.reshape(count * rows, whole.shape[2])
    crossed = lax.ppermute(own_columns(strip, parts, 1 - me), "shard", PAIR)
    theirs = lax.all_gather(crossed, "expert", axis=0, tiled=True)
    return place_halves(own_columns(weights, parts, me), theirs)


def gather_experts(weight):
    low = weight[0].astype(BF)
    if lax.axis_size("shard") != 2:
        return lax.all_gather(low, "shard", axis=0, tiled=True)
    return place_halves(low, lax.ppermute(low, "shard", PAIR))


def rms_scale(values, gain_vec):
    return values * lax.rsqrt(jnp.mean(values * values, axis=-1, keepdims=True) + NORM_EPS) * gain_vec


def rms_back(values, gain_vec, grad):
    inv = lax.rsqrt(jnp.mean(values * values, axis=-1, keepdims=True) + NORM_EPS)
    scaled = grad * gain_vec
    inner = jnp.mean(values * scaled, axis=-1, keepdims=True)
    return inv * scaled - values * (inv * inv * inv * inner), jnp.sum(grad * values * inv, axis=0)


def rotate(values, cosine, sine):
    half = values.shape[-1] // 2
    a, b = values[..., :half], values[..., half:]
    return jnp.concatenate([a * cosine - b * sine, b * cosine + a * sine], axis=-1)


def rotate_back(values, cosine, sine):
    half = values.shape[-1] // 2
    a, b = values[..., :half], values[..., half:]
    return jnp.concatenate([a * cosine + b * sine, b * cosine - a * sine], axis=-1)


def sigmoid(values):
    return 1.0 / (1.0 + jnp.exp(-values))


def doc_layout(lengths_row, order_row, count):
    slots = jnp.arange(lengths_row.shape[0], dtype=jnp.int32)
    picked = jnp.sum(jnp.where(order_row[:, None] == slots[None, :], lengths_row[None, :], 0), axis=1)
    ends = jnp.sum(jnp.where(slots[None, :] <= slots[:, None], picked[None, :], 0), axis=1)
    starts = ends - picked
    places = jnp.arange(count, dtype=jnp.int32)
    segment = jnp.sum((places[:, None] >= ends[None, :]).astype(jnp.int32), axis=1)
    begin = jnp.sum(jnp.where(segment[:, None] == slots[None, :], starts[None, :], 0), axis=1)
    return places - begin, segment


def rope_tables(position, width):
    half = width // 2
    frequency = jnp.exp(-(2.0 * jnp.arange(half, dtype=F32) / width) * math.log(10000.0))
    angles = position.astype(F32)[:, None] * frequency[None, :]
    return jnp.cos(angles), jnp.sin(angles)


def body(
    tokens,
    cotangent,
    routes,
    lengths,
    doc_order,
    attn_gain,
    query_proj,
    latent_proj,
    latent_gain,
    expand_proj,
    output_proj,
    ffn_gain,
    router_proj,
    shared_gate,
    shared_up,
    shared_down,
    expert_gate,
    expert_up,
    expert_down,
):
    shards = lax.axis_size("shard")
    me = lax.axis_index("shard")
    ranks = lax.axis_size("expert")
    rank = lax.axis_index("expert")
    rows, width = tokens.shape
    group = rows * shards
    experts = router_proj.shape[1]
    top = routes.shape[1]
    capacity = min(rows, 4 * rows * top // (3 * experts))
    heads = HEADS // shards
    hidden = shared_gate.shape[1] // shards
    scale = 1.0 / math.sqrt(NOPE_DIM + ROPE_DIM)

    low_tokens = shard_gather(tokens)
    gains = jnp.concatenate([attn_gain, ffn_gain, latent_gain]).astype(BF)[None]
    gains = shard_gather(gains).astype(F32)
    attn_part = attn_gain.shape[0]
    attn_gain_f = gains[:, :attn_part].reshape(-1)
    ffn_gain_f = gains[:, attn_part : 2 * attn_part].reshape(-1)
    latent_gain_f = gains[:, 2 * attn_part :].reshape(-1)
    router_w = shard_gather(router_proj.astype(BF))
    first_w = column_blocks(
        (query_proj, latent_proj), (heads * (NOPE_DIM + ROPE_DIM), 0)
    )
    expand_w = column_blocks((expand_proj,), (heads * (NOPE_DIM + V_DIM),))
    shared_w = column_blocks((shared_gate, shared_up), (hidden, hidden))
    low_cot = shard_gather(cotangent)
    gate_w = gather_experts(expert_gate)
    up_w = gather_experts(expert_up)
    down_w = gather_experts(expert_down)
    output_w = output_proj.astype(BF)
    shared_down_w = shared_down.astype(BF)
    cot_all = lax.all_gather(cotangent, "expert", axis=0, tiled=True)

    position, segment = doc_layout(lengths[0], doc_order[0], group)
    cosine, sine = rope_tables(position, ROPE_DIM)
    place = jnp.arange(group, dtype=jnp.int32)
    visible = (segment[:, None] == segment[None, :]) & (place[None, :] <= place[:, None])
    input_rows = tokens.astype(F32)
    normed_one = rms_scale(low_tokens.astype(F32), attn_gain_f).astype(BF)
    raw = dot(normed_one, first_w)
    query_cols = heads * (NOPE_DIM + ROPE_DIM)
    query_heads = raw[:, :query_cols].reshape(group, heads, NOPE_DIM + ROPE_DIM)
    latent_raw = raw[:, query_cols : query_cols + LATENT]
    latent = rms_scale(latent_raw, latent_gain_f).astype(BF)
    key_rope = rotate(raw[:, query_cols + LATENT :], cosine, sine).astype(BF)
    expanded = dot(latent, expand_w).astype(BF).reshape(group, heads, NOPE_DIM + V_DIM)
    keys = jnp.concatenate(
        [
            expanded[:, :, :NOPE_DIM],
            jnp.broadcast_to(key_rope[:, None, :], (group, heads, ROPE_DIM)),
        ],
        axis=-1,
    )
    values = expanded[:, :, NOPE_DIM:]
    queries = jnp.concatenate(
        [
            query_heads[:, :, :NOPE_DIM],
            rotate(query_heads[:, :, NOPE_DIM:], cosine[:, None, :], sine[:, None, :]),
        ],
        axis=-1,
    ).astype(BF)
    scores = jnp.einsum("qhd,khd->hqk", queries, keys, preferred_element_type=F32) * scale
    scores = jnp.where(visible[None], scores, MASKED)
    top_score = jnp.max(scores, axis=-1, keepdims=True)
    weights = jnp.exp(scores - top_score)
    probs = weights / jnp.sum(weights, axis=-1, keepdims=True)
    probs_low = probs.astype(BF)
    attended = (
        jnp.einsum("hqk,khd->qhd", probs_low, values, preferred_element_type=F32)
        .astype(BF)
        .reshape(group, heads * V_DIM)
    )
    resid = input_rows + shard_scatter(dot(attended, output_w))

    normed_two = rms_scale(resid, ffn_gain_f).astype(BF)
    logits = dot(normed_two, router_w)
    expert_ids = jnp.arange(experts, dtype=jnp.int32)
    chosen_mask = routes[:, :, None] == expert_ids[None, None, :]
    chosen = jnp.sum(jnp.where(chosen_mask, logits[:, None, :], 0.0), axis=-1)
    gate_exp = jnp.exp(chosen - jnp.max(chosen, axis=-1, keepdims=True))
    gates = gate_exp / jnp.sum(gate_exp, axis=-1, keepdims=True)
    gate_table = jnp.sum(jnp.where(chosen_mask, gates[:, :, None], 0.0), axis=1)
    used = jnp.sum(chosen_mask.astype(F32), axis=1)
    gate_high = gate_table.astype(BF)
    gate_rest = gate_table - gate_high.astype(F32)
    gate_mid = gate_rest.astype(BF)
    gate_low = (gate_rest - gate_mid.astype(F32)).astype(BF)
    sent = jnp.concatenate(
        [normed_two, gate_high, gate_mid, gate_low, used.astype(BF)], axis=1
    )
    sent_all = lax.all_gather(sent, "expert", axis=0, tiled=True)

    normed_two_g = shard_gather(normed_two)
    shared_raw = dot(normed_two_g, shared_w)
    shared_pre, shared_lin = shared_raw[:, :hidden], shared_raw[:, hidden:]
    shared_sig = sigmoid(shared_pre)
    shared_act = (shared_pre * shared_sig * shared_lin).astype(BF)
    shared_out = shard_scatter(dot(shared_act, shared_down_w))
    shared_act_grad = dot(low_cot, shared_down_w, ((1,), (1,)))
    shared_grads = jnp.concatenate(
        [
            shared_act_grad * shared_lin * (shared_sig * (1.0 + shared_pre * (1.0 - shared_sig))),
            shared_act_grad * (shared_pre * shared_sig),
        ],
        axis=1,
    ).astype(BF)
    shared_back = shard_scatter(dot(shared_grads, shared_w, ((1,), (1,))))
    grad_shared_pair = dot(normed_two_g, shared_grads, ((0,), (0,))).astype(BF)

    extra = sent_all[:, width:].reshape(ranks, rows, 4, experts)
    extra = lax.dynamic_index_in_dim(extra, rank, 3, keepdims=False).astype(F32)
    gate_seen = extra[:, :, 0] + extra[:, :, 1] + extra[:, :, 2]
    used_seen = extra[:, :, 3]
    earlier = (place[:rows, None] < place[None, :rows]).astype(BF)
    order = dot(used_seen.astype(BF), earlier)
    slot = jnp.where(used_seen > 0.5, order, -1.0)
    pick = slot[:, None, :] == jnp.arange(capacity, dtype=F32)[None, :, None]
    pick_low = pick.astype(BF)
    gate_slot = jnp.sum(jnp.where(pick, gate_seen[:, None, :], 0.0), axis=2)
    normed_all = sent_all[:, :width].reshape(ranks, rows, width)
    taken = (
        jnp.einsum("sct,std->scd", pick_low, normed_all, preferred_element_type=F32)
        .astype(BF)
        .reshape(ranks * capacity, width)
    )
    cot_taken = jnp.einsum(
        "sct,std->scd",
        pick_low,
        cot_all.reshape(ranks, rows, width),
        preferred_element_type=F32,
    )
    mix_grad = (gate_slot[:, :, None] * cot_taken).astype(BF).reshape(ranks * capacity, width)
    pre = dot(taken, gate_w)
    lin = dot(taken, up_w)
    sig = sigmoid(pre)
    act = (pre * sig * lin).astype(BF)
    built = dot(act, down_w).astype(BF).astype(F32).reshape(ranks, capacity, width)
    gate_grad_slot = jnp.sum(cot_taken * built, axis=2)
    gate_grad_seen = jnp.sum(jnp.where(pick, gate_grad_slot[:, :, None], 0.0), axis=1)
    gate_grad_table = lax.all_to_all(
        gate_grad_seen, "expert", split_axis=0, concat_axis=0, tiled=True
    )
    mixed = jnp.einsum(
        "sct,scd->std",
        pick_low,
        (gate_slot[:, :, None] * built).astype(BF),
        preferred_element_type=F32,
    ).astype(BF)
    mixture = lax.psum_scatter(
        mixed.reshape(ranks * rows, width), "expert", scatter_dimension=0, tiled=True
    ).astype(F32)
    act_grad = dot(mix_grad, down_w, ((1,), (1,)))
    pre_grad = (act_grad * lin * (sig * (1.0 + pre * (1.0 - sig)))).astype(BF)
    lin_grad = (act_grad * (pre * sig)).astype(BF)
    rows_grad = (
        dot(pre_grad, gate_w, ((1,), (1,))) + dot(lin_grad, up_w, ((1,), (1,)))
    ).astype(BF)
    rows_back = jnp.einsum(
        "sct,scd->std",
        pick_low,
        rows_grad.reshape(ranks, capacity, width),
        preferred_element_type=F32,
    ).astype(BF)
    normed_grad = lax.psum_scatter(
        rows_back.reshape(ranks * rows, width), "expert", scatter_dimension=0, tiled=True
    ).astype(F32)
    grad_gate_e = shard_scatter(dot(taken, pre_grad, ((0,), (0,))))[None]
    grad_up_e = shard_scatter(dot(taken, lin_grad, ((0,), (0,))))[None]
    grad_down_e = shard_scatter(dot(act, mix_grad, ((0,), (0,))))[None]

    layer_out = resid + mixture + shared_out

    upstream = cotangent.astype(F32)
    gate_grad = gate_grad_table.T
    mean_term = jnp.sum(gate_table * gate_grad, axis=-1, keepdims=True)
    logits_grad = jnp.where(used > 0.5, gate_table * (gate_grad - mean_term), 0.0).astype(BF)
    grad_router = dot(normed_two, logits_grad, ((0,), (0,)))
    normed_grad = normed_grad + dot(logits_grad, router_w, ((1,), (1,))) + shared_back
    resid_part, gain_ffn_grad = rms_back(resid, ffn_gain_f, normed_grad)
    resid_grad = upstream + resid_part
    out_grad = shard_gather(resid_grad.astype(BF))

    half_cols = width // shards
    attended_all = shard_columns(attended)
    own_out_grad = lax.dynamic_slice_in_dim(out_grad, me * half_cols, half_cols, 1)
    grad_output = dot(attended_all, own_out_grad, ((0,), (0,))).astype(BF)
    shared_act_all = shard_columns(shared_act)
    own_cot = lax.dynamic_slice_in_dim(low_cot, me * half_cols, half_cols, 1)
    grad_shared_down = dot(shared_act_all, own_cot, ((0,), (0,))).astype(BF)
    attended_grad = (
        dot(out_grad, output_w, ((1,), (1,))).astype(BF).reshape(group, heads, V_DIM)
    )
    prob_grad = jnp.einsum("qhd,khd->hqk", attended_grad, values, preferred_element_type=F32)
    row_term = jnp.sum(probs * prob_grad, axis=-1, keepdims=True)
    score_grad = (probs * (prob_grad - row_term) * scale).astype(BF)
    query_grad = jnp.einsum("hqk,khd->qhd", score_grad, keys, preferred_element_type=F32)
    key_grad = jnp.einsum("hqk,qhd->khd", score_grad, queries, preferred_element_type=F32)
    value_grad = jnp.einsum(
        "hqk,qhd->khd", probs_low, attended_grad, preferred_element_type=F32
    )
    expanded_grad = (
        jnp.concatenate([key_grad[:, :, :NOPE_DIM], value_grad], axis=-1)
        .astype(BF)
        .reshape(group, heads * (NOPE_DIM + V_DIM))
    )
    rope_grad = jnp.sum(key_grad[:, :, NOPE_DIM:], axis=1)
    grad_expand = dot(latent, expanded_grad, ((0,), (0,))).astype(BF)
    latent_part = dot(expanded_grad, expand_w, ((1,), (1,)))
    latent_sum = shard_sum(jnp.concatenate([latent_part, rope_grad], axis=1))
    latent_rms_grad, _ = rms_back(latent_raw, latent_gain_f, latent_sum[:, :LATENT])
    latent_raw_grad = jnp.concatenate(
        [latent_rms_grad, rotate_back(latent_sum[:, LATENT:], cosine, sine)], axis=-1
    ).astype(BF)
    own_rows = (place // rows == me)[:, None]
    latent_inv = lax.rsqrt(jnp.mean(latent_raw * latent_raw, axis=-1, keepdims=True) + NORM_EPS)
    gain_latent_grad = jnp.sum(
        jnp.where(own_rows, latent_sum[:, :LATENT] * latent_raw * latent_inv, 0.0), axis=0
    )
    query_raw_grad = (
        jnp.concatenate(
            [
                query_grad[:, :, :NOPE_DIM],
                rotate_back(query_grad[:, :, NOPE_DIM:], cosine[:, None, :], sine[:, None, :]),
            ],
            axis=-1,
        )
        .reshape(group, query_cols)
        .astype(BF)
    )
    own_latent = lax.dynamic_slice_in_dim(
        latent_raw_grad, me * (latent_raw_grad.shape[1] // shards), latent_raw_grad.shape[1] // shards, 1
    )
    grad_query = dot(normed_one, query_raw_grad, ((0,), (0,))).astype(BF)
    grad_latent = dot(normed_one, own_latent, ((0,), (0,))).astype(BF)
    raw_grad = jnp.concatenate(
        [query_raw_grad, jnp.where(own_rows, latent_raw_grad, jnp.zeros((), BF))], axis=1
    )
    first_grad = shard_scatter(dot(raw_grad, first_w, ((1,), (1,))))
    input_part, gain_attn_grad = rms_back(input_rows, attn_gain_f, first_grad)
    tokens_grad = resid_grad + input_part

    def spread(grad):
        return lax.psum_scatter(grad, "expert", scatter_dimension=0, tiled=True)

    shared_pair = spread(grad_shared_pair)
    shared_down_part = spread(grad_shared_down)
    output_part = spread(grad_output)
    expand_part = spread(grad_expand)
    latent_cols = spread(grad_latent)
    query_part = spread(grad_query)
    out_query = shard_transpose(query_part).astype(F32)
    out_latent = shard_transpose(latent_cols).astype(F32)
    out_expand = shard_transpose(expand_part).astype(F32)
    out_output = shard_transpose(output_part).astype(F32)
    out_gate = shard_transpose(shared_pair[:, :hidden]).astype(F32)
    out_up = shard_transpose(shared_pair[:, hidden:]).astype(F32)
    out_down = shard_transpose(shared_down_part).astype(F32)

    parts = ranks * shards
    small = jnp.concatenate(
        [
            gain_attn_grad.reshape(parts, -1),
            gain_ffn_grad.reshape(parts, -1),
            gain_latent_grad.reshape(parts, -1),
            grad_router.reshape(parts, -1),
        ],
        axis=1,
    )
    small = lax.psum_scatter(
        small, ("expert", "shard"), scatter_dimension=0, tiled=True
    ).reshape(-1)
    n_attn, n_latent = width // parts, LATENT // parts
    out_attn_gain = small[:n_attn]
    out_ffn_gain = small[n_attn : 2 * n_attn]
    out_latent_gain = small[2 * n_attn : 2 * n_attn + n_latent]
    out_router = small[2 * n_attn + n_latent :].reshape(n_attn, experts)
    return (
        layer_out,
        tokens_grad,
        out_attn_gain,
        out_query,
        out_latent,
        out_latent_gain,
        out_expand,
        out_output,
        out_ffn_gain,
        out_router,
        out_gate,
        out_up,
        out_down,
        grad_gate_e,
        grad_up_e,
        grad_down_e,
    )


def shard_columns(block):
    if lax.axis_size("shard") != 2:
        return lax.all_gather(block, "shard", axis=1, tiled=True)
    other = lax.ppermute(block, "shard", PAIR)
    first = lax.axis_index("shard") == 0
    return jnp.concatenate([jnp.where(first, block, other), jnp.where(first, other, block)], axis=1)


def solution(mesh):
    both = ("expert", "shard")
    rows, cols = P(both, None), P("shard", None)
    owned = P("expert", "shard", None)
    return jax.shard_map(
        body,
        mesh=mesh,
        in_specs=(
            rows,
            rows,
            rows,
            P("expert", None),
            P("expert", None),
            P("shard"),
            cols,
            cols,
            P("shard"),
            cols,
            cols,
            P("shard"),
            cols,
            cols,
            cols,
            cols,
            owned,
            owned,
            owned,
        ),
        out_specs=(
            rows,
            rows,
            P(both),
            rows,
            rows,
            P(both),
            rows,
            rows,
            P(both),
            rows,
            rows,
            rows,
            rows,
            owned,
            owned,
            owned,
        ),
        check_vma=False,
    )
```

time: 2980 us -> 1280 us (0.43)
  waiting for transfers between devices: 1910 us -> 805 us
  blocking collectives: 538 us -> 12 us
  matrix products: 262 us -> 211 us
    reduce_scatter x9 -> x7, waiting for transfers between devices: 1350 us -> 243 us  [the longest x5 214 us: spread(): return lax.psum_scatter(grad, 'expert', scatter_dimension=0, tiled=True)]
    unnamed x2 -> x0, blocking collectives: 511 us -> none
    ppermute x0 -> x29, waiting for transfers between devices: none -> 405 us  [the longest x3 179 us: column_blocks(): crossed = lax.ppermute(own_columns(strip, parts, 1 - me), 'shard', PAIR)]
    all_gather x10 -> x5, waiting for transfers between devices: 355 us -> 63.1 us  [the longest x3 63.1 us: column_blocks(): theirs = lax.all_gather(crossed, 'expert', axis=0, tiled=True)]
    all_to_all x4 -> x0, waiting for transfers between devices: 195 us -> none  [the longest x1 66.1 us: body(): lax.all_to_all(outbound_grad, 'expert', split_axis=0, concat_axis=0, tile...]
    unnamed x28 -> x16, waiting for transfers between devices: 11.6 us -> 94.7 us
    convert_element_type x26 -> x18, other arithmetic: 63.8 us -> 7.98 us  [the longest x1 0.96 us: body(): out_grad = shard_gather(resid_grad.astype(BF))]
    dot_general x38, matrix products: 261 us -> 207 us  [the longest x29 163 us: dot(): lax.dot_general(left, right, (dims, ((), ())), preferred_element_type=F32)]
  transfers between devices with their start and end apart: 29 -> 43, of which waited for: 16 -> 24; matrix products, arithmetic and copies ran while one was open for 28% -> 28% of each run, Pallas kernels for 0% -> 0%
where the time goes in v1:
time: 1280 us; the launch traced here: 1270 us
  waiting for transfers between devices  805 us (63%)
  matrix products  211 us (16%)
  local copies, waits for them, and re-layouts  128 us (10%)
  other arithmetic  77.2 us (6%)
  starting transfers between devices  19.5 us (2%)
  between operations  15.9 us (1%)
    reduce_scatter x5, waiting for transfers between devices, spread(): return lax.psum_scatter(grad, 'expert', scatter_dimension=0, tiled=True)  214 us
    ppermute x3, waiting for transfers between devices, column_blocks(): crossed = lax.ppermute(own_columns(strip, parts, 1 - me), 'shard', PAIR)  179 us
    ppermute x7, waiting for transfers between devices, shard_transpose(): got = lax.ppermute(theirs, 'shard', PAIR)  173 us
    dot_general x29, matrix products, dot(): lax.dot_general(left, right, (dims, ((), ())), preferred_element_type=F32)  163 us
    unnamed x16, waiting for transfers between devices  94.7 us
    all_gather x3, waiting for transfers between devices, column_blocks(): theirs = lax.all_gather(crossed, 'expert', axis=0, tiled=True)  63.1 us
    ppermute x6, waiting for transfers between devices, shard_gather(): other = lax.ppermute(block, 'shard', PAIR)  33.4 us
    unnamed x225, local copies, waits for them, and re-layouts  28.4 us
  transfers between devices with their start and end apart: 43, of which 24 were waited for; matrix products, arithmetic and copies ran while one was open for 28% of the time, Pallas kernels for 0%

profile of v1, /device:TPU:11, one launch (start us, length us, event | category | flops | bytes accessed | tf_op | source)
XLA Modules:
  0.0 1269.0 jit_solution(7202382943565615833)
XLA Ops:
  42.4 9.6 all-gather.8.cloned.1.call-done
  53.3 53.4 %all-gather.6.cloned.1.call-done = bf16[1024,2112]{1,0:T(8,128)(2,1)} async-done(((bf16[64,2112]{1,0:T(8,128)(2,1)}), bf16[1024,2112]{1,0:T(8,128)(2,1)}) %all-gather.6.cloned.1.call-update) | async-done | bytes 4325392 | tf_op jit(solution)/shard_map/all_gather | solution.py:98
  143.6 12.4 collective-permute-done.5
  187.2 170.1 %collective-permute-done.10 = bf16[64,1408]{1,0:T(8,128)(2,1)S(1)} collective-permute-done((bf16[64,1408]{1,0:T(8,128)(2,1)S(1)}, bf16[64,1408]{1,0:T(8,128)(2,1)S(1)}, u32[]{:S(2)}, u32[]{:S(2)}) %collective-permute-start.10) | collective-permute-done | bytes 180256 | tf_op jit(solution)/shard_map/ppermute | solution.py:97
  370.8 8.5 slice.185
  390.7 12.8 %multiply_convert_fusion.3 = (bf16[1024,1408]{1,0:T(8,128)(2,1)S(1)}, f32[1024,1408]{1,0:T(8,128)}) fusion(f32[1024,1408]{1,0:T(8,128)S(1)} %fusion.143, bf16[1024,2048]{1,0:T(8,128)(2,1)S(1)} %bitcast.130, bf16[2048,1408]{1,0:T(8,128)(2,1)} %constant_dynamic-update-slice_fusion.3), kind=kOutput, calls=%fused_computation.19 | convolution fusion | flops 5914230784 | bytes 24379392 | tf_op jit(solution)/shard_map/dot_general | solution.py:21
  405.1 11.0 convolution_convert_fusion.6
  424.5 15.9 %multiply_convert_fusion.2 = (bf16[1024,1408]{1,0:T(8,128)(2,1)}, bf16[1024,1408]{1,0:T(8,128)(2,1)}) fusion(f32[1024,1408]{1,0:T(8,128)} %copy-done.92, f32[1024,1408]{1,0:T(8,128)} %get-tuple-element.178, bf16[1024,2048]{1,0:T(8,128)(2,1)S(1)} %bitcast.150, bf16[1408,2048]{1,0:T(8,128)(2,1)} %constant_dynamic-update-slice_fusion.1), kind=kOutput, calls=%fused_computation.18 | convolution fusion | flops 5924323328 | bytes 27262976 | tf_op jit(solution)/shard_map/dot_general | solution.py:21
  440.4 9.8 fusion.144
  450.2 8.4 add_convert_fusion
  496.4 7.5 collective-permute-done.24
  512.9 8.0 convolution_convert_fusion.3
  528.2 12.0 all_to_all.12
  540.8 28.4 %reduce-scatter.13.cloned.1.call-done = bf16[128,2048]{1,0:T(8,128)(2,1)} async-done(((bf16[2048,2048]{1,0:T(8,128)(2,1)}), bf16[128,2048]{1,0:T(8,128)(2,1)}) %reduce-scatter.13.cloned.1.call-update) | async-done | bytes 524304 | tf_op jit(solution)/shard_map/reduce_scatter | solution.py:339
  574.6 11.8 collective-permute-done.14
  659.7 9.3 collective-permute-done.20
  685.4 12.1 fusion.147
  697.5 9.7 fusion.146
  740.1 162.2 %collective-permute-done.22 = bf16[64,704]{1,0:T(8,128)(2,1)S(1)} collective-permute-done((bf16[64,704]{1,0:T(8,128)(2,1)S(1)}, bf16[64,704]{1,0:T(8,128)(2,1)S(1)}, u32[]{:S(2)}, u32[]{:S(2)}) %collective-permute-start.22) | collective-permute-done | bytes 90144 | tf_op jit(solution)/shard_map/ppermute | solution.py:61
  929.7 31.2 %all-reduce.3.cloned.1.call-done = f32[32,1168]{1,0:T(8,128)} async-done(((f32[32,1168]{1,0:T(8,128)}), f32[32,1168]{1,0:T(8,128)}) %all-reduce.3.cloned.1.call-update) | async-done | bytes 149520
  962.2 62.7 %reduce-scatter.25.cloned.1.call-done = bf16[128,288]{1,0:T(8,128)(2,1)} async-done(((bf16[2048,288]{1,0:T(8,128)(2,1)}), bf16[128,288]{1,0:T(8,128)(2,1)}) %reduce-scatter.25.cloned.1.call-update) | async-done | bytes 73744
  1029.3 59.8 %reduce-scatter.17.cloned.1.call-done = bf16[32,2048]{1,0:T(8,128)(2,1)} async-done(((bf16[512,2048]{1,0:T(8,128)(2,1)}), bf16[32,2048]{1,0:T(8,128)(2,1)}) %reduce-scatter.17.cloned.1.call-update) | async-done | bytes 131088 | tf_op jit(solution)/shard_map/reduce_scatter | solution.py:418
  1094.0 71.0 %reduce-scatter.19.cloned.1.call-done = bf16[128,1024]{1,0:T(8,128)(2,1)} async-done(((bf16[2048,1024]{1,0:T(8,128)(2,1)}), bf16[128,1024]{1,0:T(8,128)(2,1)}) %reduce-scatter.19.cloned.1.call-update) | async-done | bytes 262160 | tf_op jit(solution)/shard_map/reduce_scatter | solution.py:418
  1170.7 83.5 %reduce-scatter.15.cloned.1.call-done = bf16[128,1536]{1,0:T(8,128)(2,1)} async-done(((bf16[2048,1536]{1,0:T(8,128)(2,1)}), bf16[128,1536]{1,0:T(8,128)(2,1)}) %reduce-scatter.15.cloned.1.call-update) | async-done | bytes 393232 | tf_op jit(solution)/shard_map/reduce_scatter | solution.py:418
  (500 shorter events, 371.8 us)
Async XLA Ops:
  7.2 44.8 %all-gather.8.cloned.1.call-start = ((), (), s32[]{:S(2)}) async-start(), calls=%async_computation.10 | async-start | bytes 1114112 | tf_op jit(solution)/shard_map/all_gather | solution.py:98
  12.1 94.6 %all-gather.6.cloned.1.call-start = ((), (), s32[]{:S(2)}) async-start(), calls=%async_computation.9 | async-start | bytes 4734976 | tf_op jit(solution)/shard_map/all_gather | solution.py:98
  21.7 347.5 %all-gather.10.cloned.1.call-start = ((), (), s32[]{:S(2)}) async-start(), calls=%async_computation.11 | async-start | bytes 9469952 | tf_op jit(solution)/shard_map/all_gather | solution.py:266
  160.9 255.3 %all-gather.14.cloned.1.call-start = ((), (), s32[]{:S(2)}) async-start(), calls=%async_computation.14 | async-start | bytes 8912896 | tf_op jit(solution)/shard_map/all_gather | solution.py:207
  161.4 316.4 %all-gather.12.cloned.1.call-start = ((), (), s32[]{:S(2)}) async-start(), calls=%async_computation.13 | async-start | bytes 3063808 | tf_op jit(solution)/shard_map/all_gather | solution.py:98
  166.8 191.3 %collective-permute-start.6 = (bf16[1024,1408]{1,0:T(8,128)(2,1)}, bf16[1024,1408]{1,0:T(8,128)(2,1)}, u32[]{:S(2)}, u32[]{:S(2)}) collective-permute-start(bf16[1024,1408]{1,0:T(8,128)(2,1)} %get-tuple-element.109), channel_id=1, source_target_pairs={{0,1},{1,0},{2,3},{3,2},{4,5},{5,4},{6,7},{7,6},{8,9},{9,8},{10,11... | collective-permute-start | bytes 8650760 | tf_op jit(solution)/shard_map/ppermute | solution.py:106
  174.0 187.7 %collective-permute-start.7 = (bf16[1024,1408]{1,0:T(8,128)(2,1)}, bf16[1024,1408]{1,0:T(8,128)(2,1)}, u32[]{:S(2)}, u32[]{:S(2)}) collective-permute-start(bf16[1024,1408]{1,0:T(8,128)(2,1)} %get-tuple-element.111), channel_id=1, source_target_pairs={{0,1},{1,0},{2,3},{3,2},{4,5},{5,4},{6,7},{7,6},{8,9},{9,8},{10,11... | collective-permute-start | bytes 8650760 | tf_op jit(solution)/shard_map/ppermute | solution.py:106
  183.5 181.9 %collective-permute-start.8 = (bf16[704,2048]{1,0:T(8,128)(2,1)}, bf16[704,2048]{1,0:T(8,128)(2,1)}, u32[]{:S(2)}, u32[]{:S(2)}) collective-permute-start(bf16[704,2048]{1,0:T(8,128)(2,1)} %get-tuple-element.107), channel_id=1, source_target_pairs={{0,1},{1,0},{2,3},{3,2},{4,5},{5,4},{6,7},{7,6},{8,9},{9,8},{10,11... | collective-permute-start | bytes 8650760 | tf_op jit(solution)/shard_map/ppermute | solution.py:106
  186.8 170.5 %collective-permute-start.10 = (bf16[64,1408]{1,0:T(8,128)(2,1)S(1)}, bf16[64,1408]{1,0:T(8,128)(2,1)S(1)}, u32[]{:S(2)}, u32[]{:S(2)}) collective-permute-start(bf16[64,1408]{1,0:T(8,128)(2,1)S(1)} %pad_maximum_fusion.30), channel_id=1, source_target_pairs={{0,1},{1,0},{2,3},{3,2},{4,5},{5,4},{6,7},{7,6},{8,9},{9,8},{10,11... | collective-permute-start | bytes 540680 | tf_op jit(solution)/shard_map/ppermute | solution.py:97
  358.0 211.2 %reduce-scatter.13.cloned.1.call-start = ((), (), s32[]{:S(2)}) async-start(), calls=%async_computation.15 | async-start | bytes 8912896 | tf_op jit(solution)/shard_map/reduce_scatter | solution.py:339
  464.4 215.1 %reduce-scatter.23.cloned.1.call-start = ((), (), s32[]{:S(2)}) async-start(), calls=%async_computation.20 | async-start | bytes 3063808 | tf_op jit(solution)/shard_map/reduce_scatter | solution.py:418
  506.7 229.8 %reduce-scatter.21.cloned.1.call-start = ((), (), s32[]{:S(2)}) async-start(), calls=%async_computation.19 | async-start | bytes 6127616 | tf_op jit(solution)/shard_map/reduce_scatter | solution.py:418
  512.2 413.5 %reduce-scatter.11.cloned.1.call-start = ((), (), s32[]{:S(2)}) async-start(), calls=%async_computation.12 | async-start | bytes 8912896 | tf_op jit(solution)/shard_map/reduce_scatter | solution.py:324
  520.9 440.0 %all-reduce.3.cloned.1.call-start = ((), (), s32[]{:S(2)}) async-start(), calls=%async_computation.22 | async-start | bytes 327680
  649.2 375.8 %reduce-scatter.25.cloned.1.call-start = ((), (), s32[]{:S(2)}) async-start(), calls=%async_computation.21 | async-start | bytes 1671168
  654.8 434.3 %reduce-scatter.17.cloned.1.call-start = ((), (), s32[]{:S(2)}) async-start(), calls=%async_computation.17 | async-start | bytes 2228224 | tf_op jit(solution)/shard_map/reduce_scatter | solution.py:418
  658.5 506.5 %reduce-scatter.19.cloned.1.call-start = ((), (), s32[]{:S(2)}) async-start(), calls=%async_computation.18 | async-start | bytes 4456448 | tf_op jit(solution)/shard_map/reduce_scatter | solution.py:418
  674.5 579.7 %reduce-scatter.15.cloned.1.call-start = ((), (), s32[]{:S(2)}) async-start(), calls=%async_computation.16 | async-start | bytes 6684672 | tf_op jit(solution)/shard_map/reduce_scatter | solution.py:418
  716.7 189.5 %collective-permute-start.27 = (bf16[1024,1408]{1,0:T(8,128)(2,1)}, bf16[1024,1408]{1,0:T(8,128)(2,1)}, u32[]{:S(2)}, u32[]{:S(2)}) collective-permute-start(bf16[1024,1408]{1,0:T(8,128)(2,1)} %dynamic-slice_convert_fusion.2), channel_id=1, source_target_pairs={{0,1},{1,0},{2,3},{3,2},{4,5},{5,4},{6,7},{7,6},{8,9},{9,8},{10,11... | collective-permute-start | bytes 8650760 | tf_op jit(solution)/shard_map/ppermute | solution.py:42
  722.5 190.7 %collective-permute-start.26 = (bf16[1024,1408]{1,0:T(8,128)(2,1)}, bf16[1024,1408]{1,0:T(8,128)(2,1)}, u32[]{:S(2)}, u32[]{:S(2)}) collective-permute-start(bf16[1024,1408]{1,0:T(8,128)(2,1)} %dynamic-slice_convert_fusion.3), channel_id=1, source_target_pairs={{0,1},{1,0},{2,3},{3,2},{4,5},{5,4},{6,7},{7,6},{8,9},{9,8},{10,11... | collective-permute-start | bytes 8650760 | tf_op jit(solution)/shard_map/ppermute | solution.py:42
  735.5 184.5 %collective-permute-start.28 = (bf16[704,2048]{1,0:T(8,128)(2,1)}, bf16[704,2048]{1,0:T(8,128)(2,1)}, u32[]{:S(2)}, u32[]{:S(2)}) collective-permute-start(bf16[704,2048]{1,0:T(8,128)(2,1)} %dynamic-slice_convert_fusion.1), channel_id=1, source_target_pairs={{0,1},{1,0},{2,3},{3,2},{4,5},{5,4},{6,7},{7,6},{8,9},{9,8},{10,11... | collective-permute-start | bytes 8650760 | tf_op jit(solution)/shard_map/ppermute | solution.py:42
  737.8 164.5 %collective-permute-start.22 = (bf16[64,704]{1,0:T(8,128)(2,1)S(1)}, bf16[64,704]{1,0:T(8,128)(2,1)S(1)}, u32[]{:S(2)}, u32[]{:S(2)}) collective-permute-start(bf16[64,704]{1,0:T(8,128)(2,1)S(1)} %constant_dynamic-slice_fusion.2), channel_id=1, source_target_pairs={{0,1},{1,0},{2,3},{3,2},{4,5},{5,4},{6,7},{7,6},{8,9},{9,8},{10,11... | collective-permute-start | bytes 270344 | tf_op jit(solution)/shard_map/ppermute | solution.py:61
  738.2 166.1 %collective-permute-start.23 = (bf16[64,704]{1,0:T(8,128)(2,1)S(1)}, bf16[64,704]{1,0:T(8,128)(2,1)S(1)}, u32[]{:S(2)}, u32[]{:S(2)}) collective-permute-start(bf16[64,704]{1,0:T(8,128)(2,1)S(1)} %constant_dynamic-slice_fusion.1), channel_id=1, source_target_pairs={{0,1},{1,0},{2,3},{3,2},{4,5},{5,4},{6,7},{7,6},{8,9},{9,8},{10,11... | collective-permute-start | bytes 270344 | tf_op jit(solution)/shard_map/ppermute | solution.py:61
  902.3 23.4 %collective-permute-start.11 = (bf16[128,2048]{1,0:T(8,128)(2,1)}, bf16[128,2048]{1,0:T(8,128)(2,1)}, u32[]{:S(2)}, u32[]{:S(2)}) collective-permute-start(bf16[128,2048]{1,0:T(8,128)(2,1)} %dynamic-slice_convert_fusion.9), channel_id=1, source_target_pairs={{0,1},{1,0},{2,3},{3,2},{4,5},{5,4},{6,7},{7,6},{8,9},{9,8},{10,11... | collective-permute-start | bytes 1572872 | tf_op jit(solution)/shard_map/ppermute | solution.py:42
  (126 other events, 1925.2 us)
Sparse Core Ops, SparseCore 0:
  12.2 39.7 all-gather.7
  54.9 51.8 all-gather.5
  161.0 76.7 all-gather.9
  239.8 73.2 all-gather.13
  358.2 44.5 all-gather.11
  464.5 104.7 reduce-scatter.12
  573.6 62.5 reduce-scatter.22
  641.2 81.8 reduce-scatter.20
  727.7 104.8 reduce-scatter.10
  839.5 121.4 all-reduce.2
  965.0 59.8 reduce-scatter.24
  1028.5 60.5 reduce-scatter.16
  1093.5 71.4 reduce-scatter.18
  1168.7 85.3 reduce-scatter.14
